TPU v7x, 32 devices: a whole 2x2x4 slice. The times are simulated.
32 devices in a mesh: light: 16 (over z, y, x), pair: 2 (over core).
Axes of the slice: x: 2, y: 2, z: 4, core: 2. Of those that a mesh axis runs over, the one named last changes fastest.
Arguments:
- tokens: bfloat16 [32768, 2048], P(('light', 'pair')), may hold values from -36 to 36
- norm_gain: float32 [2048], replicated, may hold values from 0.1 to 1.9
- light_gate: bfloat16 [2048, 1280], P(None, 'pair'), may hold values from -0.125 to 0.125
- light_up: bfloat16 [2048, 1280], P(None, 'pair'), may hold values from -0.125 to 0.125
- light_down: bfloat16 [1280, 2048], P('pair'), may hold values from -0.15625 to 0.15625
- heavy_gate: bfloat16 [2048, 10240], P(None, 'light'), may hold values from -0.125 to 0.125
- heavy_up: bfloat16 [2048, 10240], P(None, 'light'), may hold values from -0.125 to 0.125
- heavy_down: bfloat16 [10240, 2048], P('light'), may hold values from -0.0625 to 0.0625
- slot_token_index: int32 [1024], P(('light', 'pair')), may hold values from 0 to 1023, as said below
- slot_active_mask: int32 [1024], P(('light', 'pair')), may hold values from 0 to 1, as said below
Outputs:
- mixed: bfloat16 [32768, 2048], P(('light', 'pair'))
Inputs may be any that keep to these rules, and one draw needn't show every extreme that they name: `slot_token_index`: entry s belongs to device s // 32 in the order of light+pair; the live slots of one device name distinct tokens of that device, as positions among its 1024 tokens. `slot_active_mask`: every device has at least one live slot; in every draw some device has all 32 of its slots live.
All inputs are finite; a program needn't handle non-finite values.
Results may differ from a plain program's by a relative error of at most 0.0044.
Values may be sent and summed in bfloat16 or wider, within the bound.
A program may use at most 192 MiB of HBM per device.

v0:
```python
import jax
import jax.numpy as jnp
from jax import lax
from jax.sharding import PartitionSpec as P

epsilon = 1e-06


def gated_units(rows, w_gate, w_up):
    gate = jnp.dot(rows, w_gate, preferred_element_type=jnp.float32)
    upward = jnp.dot(rows, w_up, preferred_element_type=jnp.float32)
    return (jax.nn.silu(gate) * upward).astype(jnp.bfloat16)


def body(
    tokens,
    norm_gain,
    light_gate,
    light_up,
    light_down,
    heavy_gate,
    heavy_up,
    heavy_down,
    slot_token_index,
    slot_active_mask,
):
    residual = tokens.astype(jnp.float32)
    mean_square = jnp.mean(residual * residual, axis=-1, keepdims=True)
    normalized_input = (residual * lax.rsqrt(mean_square + epsilon) * norm_gain).astype(
        jnp.bfloat16
    )
    slot_count = slot_token_index.shape[0]
    tok_count = tokens.shape[0]
    active_flags = slot_active_mask.astype(jnp.bfloat16)[:, None]
    routed_output = jnp.take(normalized_input, slot_token_index, axis=0) * active_flags
    heavy_hidden = gated_units(
        lax.all_gather(routed_output, "light", axis=0, tiled=True), heavy_gate, heavy_up
    )
    paired_rows = lax.all_gather(normalized_input, "pair", axis=0, tiled=True)
    light_hidden = gated_units(paired_rows, light_gate, light_up)
    partial_out = jnp.dot(light_hidden, light_down, preferred_element_type=jnp.float32)
    light_out = lax.psum_scatter(partial_out, "pair", scatter_dimension=0, tiled=True)
    heavy_out = lax.psum_scatter(
        jnp.dot(heavy_hidden, heavy_down, preferred_element_type=jnp.float32),
        "light",
        scatter_dimension=0,
        tiled=True,
    )
    positions = lax.broadcasted_iota(jnp.int32, (tok_count, slot_count), 0)
    placing = ((positions == slot_token_index[None, :]) & (slot_active_mask[None, :] == 1)).astype(
        jnp.float32
    )
    routed_sum = jnp.dot(
        placing, heavy_out, precision=lax.Precision.HIGHEST, preferred_element_type=jnp.float32
    )
    return (residual + light_out + routed_sum).astype(jnp.bfloat16)


def solution(mesh):
    placed = (
        P(("light", "pair"), None),
        P(),
        P(None, "pair"),
        P(None, "pair"),
        P("pair", None),
        P(None, "light"),
        P(None, "light"),
        P("light", None),
        P(("light", "pair")),
        P(("light", "pair")),
    )
    return jax.shard_map(
        body, mesh=mesh, in_specs=placed, out_specs=P(("light", "pair"), None), check_vma=False
    )
```

profile of v0, /device:TPU:8, one launch (start us, length us, event | category | flops | bytes accessed | tf_op | source)
XLA Modules:
  0.0 243.5 jit_solution(2259905186288709330)
XLA Ops:
  6.5 0.8 compare_and_fusion
  7.4 1.2 compare_select_fusion
  8.6 0.7 convert_element_type.22
  9.3 3.1 %fusion = f32[1024]{0:T(1024)S(1)} fusion(bf16[1024,2048]{1,0:T(8,128)(2,1)} %param.10), kind=kLoop, calls=%fused_computation.4 | loop fusion | flops 6290432 | bytes 4198400 | tf_op jit(solution)/shard_map/reduce_sum | solution.py:28
  12.4 3.0 %fusion.2 = bf16[1024,2048]{1,0:T(8,128)(2,1)} fusion(bf16[1024,2048]{1,0:T(8,128)(2,1)S(1)} %copy-done.2, f32[2048]{0:T(1024)S(1)} %copy-done.3, f32[1024]{0:T(1024)S(1)} %add_rsqrt_fusion), kind=kLoop, calls=%fused_computation.6 | loop fusion | flops 8388608 | bytes 8400896 | tf_op jit(solution)/shard_map/convert_element_type | solution.py:29
  15.4 3.5 %gather_fusion = bf16[32,2048]{1,0:T(8,128)(2,1)S(1)} fusion(bf16[1024,2048]{1,0:T(8,128)(2,1)} %fusion.2, s32[1024]{0:T(1024)S(1)} %pad_clamp_fusion), kind=kCustom, calls=%fused_computation | custom fusion | bytes 262272 | tf_op jit(solution)/shard_map/jit(_take)/gather | solution.py:35
  18.9 0.7 select_multiply_fusion
  19.7 0.0 all-gather.5.cloned.1.call-update
  19.7 0.0 all-gather.3.cloned.1.call-start
  19.8 0.7 all-gather.3.cloned.1.call-update
  20.5 0.0 reduce-scatter.5.cloned.1.call-start
  20.5 61.3 %all-gather.5.cloned.1.call-done = bf16[512,2048]{1,0:T(8,128)(2,1)} async-done(((bf16[32,2048]{1,0:T(8,128)(2,1)}), bf16[512,2048]{1,0:T(8,128)(2,1)}) %all-gather.5.cloned.1.call-update) | async-done | bytes 2097168 | tf_op jit(solution)/shard_map/all_gather | solution.py:37
  81.8 5.2 %fusion.15 = f32[512,640]{1,0:T(8,128)} fusion(bf16[512,2048]{1,0:T(8,128)(2,1)} %all-gather.5.cloned.1.call-done, bf16[2048,640]{1,0:T(8,128)(2,1)} %param.15), kind=kOutput, calls=%fused_computation.27 | convolution fusion | flops 1342177280 | bytes 6029312 | tf_op jit(solution)/shard_map/dot_general | solution.py:10
  87.0 11.4 %fusion.6 = f32[512,2048]{1,0:T(8,128)} fusion(bf16[640,2048]{1,0:T(8,128)(2,1)} %param.17, bf16[512,2048]{1,0:T(8,128)(2,1)} %all-gather.5.cloned.1.call-done, bf16[2048,640]{1,0:T(8,128)(2,1)} %param.16, f32[512,640]{1,0:T(8,128)} %fusion.15), kind=kOutput, calls=%fused_computation.12 | convolution fusion | flops 2686320640 | bytes 12845056 | tf_op jit(solution)/shard_map/dot_general | solution.py:44
  98.4 0.0 reduce-scatter.5.cloned.1.call-update
  98.4 0.2 reduce-scatter.3.cloned.1.call-start
  98.7 3.4 %all-gather.3.cloned.1.call-done = bf16[2048,2048]{1,0:T(8,128)(2,1)} async-done(((bf16[1024,2048]{1,0:T(8,128)(2,1)}), bf16[2048,2048]{1,0:T(8,128)(2,1)}) %all-gather.3.cloned.1.call-update) | async-done | bytes 8388624 | tf_op jit(solution)/shard_map/all_gather | solution.py:39
  102.1 11.4 %fusion.13 = f32[2048,640]{1,0:T(8,128)} fusion(bf16[2048,2048]{1,0:T(8,128)(2,1)} %all-gather.3.cloned.1.call-done, bf16[2048,640]{1,0:T(8,128)(2,1)} %param.12), kind=kOutput, calls=%fused_computation.25 | convolution fusion | flops 5368709120 | bytes 16252928 | tf_op jit(solution)/shard_map/dot_general | solution.py:10
  113.5 22.2 %fusion.14 = f32[2048,2048]{1,0:T(8,128)} fusion(bf16[640,2048]{1,0:T(8,128)(2,1)S(1)} %copy-done, f32[2048,640]{1,0:T(8,128)} %fusion.13, bf16[2048,2048]{1,0:T(8,128)(2,1)} %all-gather.3.cloned.1.call-done, bf16[2048,640]{1,0:T(8,128)(2,1)} %param.13), kind=kOutput, calls=%fused_computation.26 | convolution fusion | flops 10745282560 | bytes 35651584 | tf_op jit(solution)/shard_map/dot_general | solution.py:41
  135.8 0.0 reduce-scatter.3.cloned.1.call-update
  135.8 0.6 copy-done.5
  136.4 62.1 %reduce-scatter.5.cloned.1.call-done = f32[32,2048]{1,0:T(8,128)} async-done(((f32[512,2048]{1,0:T(8,128)}), f32[32,2048]{1,0:T(8,128)}) %reduce-scatter.5.cloned.1.call-update) | async-done | bytes 262160 | tf_op jit(solution)/shard_map/reduce_scatter | solution.py:43
  198.5 30.3 %reduce-scatter.3.cloned.1.call-done = f32[1024,2048]{1,0:T(8,128)} async-done(((f32[2048,2048]{1,0:T(8,128)}), f32[1024,2048]{1,0:T(8,128)}) %reduce-scatter.3.cloned.1.call-update) | async-done | bytes 8388624 | tf_op jit(solution)/shard_map/reduce_scatter | solution.py:42
  228.8 8.2 %fusion.4 = bf16[1024,2048]{1,0:T(8,128)(2,1)} fusion(f32[1024,2048]{1,0:T(8,128)} %reduce-scatter.3.cloned.1.call-done, bf16[1024,2048]{1,0:T(8,128)(2,1)} %param.10, f32[32,2048]{1,0:T(8,128)} %reduce-scatter.5.cloned.1.call-done, s32[32]{0:T(128)S(1)} %copy-done.4, pred[32]{0:T(512)(128)(4,1)S(1)} %broadcast_compare_fusion), kind=kOutput, calls=%fused_computation.8 | convolution fusion | flops 813760512 | bytes 17039520 | tf_op jit(solution)/shard_map/dot_general | solution.py:53
  (15 shorter events, 0.0 us)
Async XLA Ops:
  6.5 107.0 %copy-start = (bf16[640,2048]{1,0:T(8,128)(2,1)S(1)}, bf16[640,2048]{1,0:T(8,128)(2,1)}, u32[]{:S(2)}) copy-start(bf16[640,2048]{1,0:T(8,128)(2,1)} %param.14) | copy-start | bytes 7864324
  6.5 5.8 %copy-start.3 = (f32[2048]{0:T(1024)S(1)}, f32[2048]{0:T(1024)}, u32[]{:S(2)}) copy-start(f32[2048]{0:T(1024)} %param.11) | copy-start | bytes 24580
  6.5 75.2 %all-gather.5.cloned.1.call-start = ((), (), s32[]{:S(2)}) async-start(), calls=%async_computation.4 | async-start | bytes 2228224 | tf_op jit(solution)/shard_map/all_gather | solution.py:37
  6.5 5.9 %copy-start.2 = (bf16[1024,2048]{1,0:T(8,128)(2,1)S(1)}, bf16[1024,2048]{1,0:T(8,128)(2,1)}, u32[]{:S(2)}) copy-start(bf16[1024,2048]{1,0:T(8,128)(2,1)} %param.10) | copy-start | bytes 12582916
  19.7 82.4 %all-gather.3.cloned.1.call-start = ((), (), s32[]{:S(2)}) async-start(), calls=%async_computation.2 | async-start | bytes 12582912 | tf_op jit(solution)/shard_map/all_gather | solution.py:39
  20.5 178.0 %reduce-scatter.5.cloned.1.call-start = ((), (), s32[]{:S(2)}) async-start(), calls=%async_computation.5 | async-start | bytes 4456448 | tf_op jit(solution)/shard_map/reduce_scatter | solution.py:43
  98.4 130.3 %reduce-scatter.3.cloned.1.call-start = ((), (), s32[]{:S(2)}) async-start(), calls=%async_computation.3 | async-start | bytes 25165824 | tf_op jit(solution)/shard_map/reduce_scatter | solution.py:42
  135.8 0.7 copy-start.5
  135.8 93.0 %copy-start.4 = (s32[32]{0:T(128)S(1)}, s32[32]{0:T(128)}, u32[]{:S(2)}) copy-start(s32[32]{0:T(128)} %param.18) | copy-start | bytes 388
  228.8 8.2 %copy-start.1 = (bf16[640,2048]{1,0:T(8,128)(2,1)S(1)}, bf16[640,2048]{1,0:T(8,128)(2,1)}, u32[]{:S(2)}) copy-start(bf16[640,2048]{1,0:T(8,128)(2,1)} %param.14) | copy-start | bytes 7864324
Sparse Core Ops, SparseCore 0:
  19.8 61.9 all-gather.4
  83.3 18.7 all-gather.2
  104.4 94.0 reduce-scatter.4
  200.6 28.1 reduce-scatter.2
where the time goes:
time: 245 us; the launch traced here: 243 us
  waiting for transfers between devices  158 us (64%)
  matrix products  58.5 us (24%)
  between operations  13.2 us (5%)
  other arithmetic  9.61 us (4%)
  local copies, waits for them, and re-layouts  4.14 us (2%)
    reduce_scatter x1, waiting for transfers between devices, body(): lax.psum_scatter(jnp.dot(heavy_hidden, heavy_down, preferred_element_type...  62.1 us
    all_gather x1, waiting for transfers between devices, body(): lax.all_gather(routed_output, 'light', axis=0, tiled=True)  61.3 us
    reduce_scatter x1, waiting for transfers between devices, body(): lax.psum_scatter(partial_out, 'pair', scatter_dimension=0, tiled=True)  30.3 us
    dot_general x1, matrix products, body(): jnp.dot(light_hidden, light_down, preferred_element_type=jnp.float32)  22.2 us
    dot_general x2, matrix products, gated_units(): gate = jnp.dot(rows, w_gate, preferred_element_type=jnp.float32)  16.7 us
    dot_general x1, matrix products, body(): jnp.dot(heavy_hidden, heavy_down, preferred_element_type=jnp.float32)  11.4 us
    dot_general x1, matrix products, body(): jnp.dot(placing, heavy_out, precision=lax.Precision.HIGHEST, preferred_el...  8.18 us
  transfers between devices with their start and end apart: 4, of which 4 were waited for; matrix products, arithmetic and copies ran while one was open for 21% of the time, Pallas kernels for 0%

commit v1 on v0

v1 whole, which is shorter than its diff:
```python
import functools

import jax
import jax.numpy as jnp
from jax import lax
from jax.experimental import pallas as pl
from jax.experimental.pallas import tpu as pltpu
from jax.sharding import PartitionSpec as P

epsilon = 1e-06
MESH = pl.DeviceIdType.MESH
F32, BF16 = jnp.float32, jnp.bfloat16
ORDERS = ((0, 1, 2), (0, 2, 1))


def three_factors(n):
    dims, left = [], n
    for power in (3, 2, 1):
        f = 1
        while f**power < left or left % f:
            f += 1
        dims.append(f)
        left //= f
    return tuple(dims)


def kth_nearest(k, x, length):
    if k == 0:
        return x
    if length == 2:
        return 1 - x
    reach = jnp.minimum(x, length - 1 - x)
    sign = jnp.where(2 * x < length, 1, -1)
    both = k <= 2 * reach
    distance = jnp.where(both, (k + 1) // 2, k - reach)
    return x + distance * jnp.where(both, sign * (1 if k % 2 else -1), sign)


class Plan:
    def __init__(self, dims, me):
        self.dims = dims
        a, b, c = dims
        self.my = (me // (b * c), me // c % b, me % c)
        self.slots = []
        self.base = []
        for order in ORDERS:
            base, total, before = [], 0, 1
            for dim in order:
                base.append(total)
                length = dims[dim]
                total += before if length == 2 else before * (length + 1)
                before *= length
            self.base.append(base)
            self.slots.append(total)

    def events(self, h):
        a, p, q = (self.dims[d] for d in ORDERS[h])
        every = [(i, j, k) for i in range(a) for j in range(p) for k in range(q)]
        every.sort(key=lambda e: (e[2], e[0] + e[1], e[1]))
        return every[1:]

    def token(self, h, e):
        t = [None] * 3
        for lvl, dim in enumerate(ORDERS[h]):
            t[dim] = kth_nearest(e[lvl], self.my[dim], self.dims[dim])
        return tuple(t)

    def index(self, t):
        return (t[0] * self.dims[1] + t[1]) * self.dims[2] + t[2]

    def place(self, t, at):
        a, b, c = self.dims
        group = (t[1] - at[1] + b) % b * c + (t[2] - at[2] + c) % c
        return (group + b * c - 1) % (b * c) * a + t[0]

    def top(self, e):
        return max([-1] + [lvl for lvl in range(3) if e[lvl]])

    def moved(self, dim, x):
        at = list(self.my)
        at[dim] = x
        return tuple(at)

    def children(self, h, e):
        t, top, out = self.token(h, e), self.top(e), []
        for lvl in range(max(top, 0), 3):
            dim = ORDERS[h][lvl]
            length, x = self.dims[dim], self.my[dim]
            if length == 1:
                continue
            if lvl == top:
                if length > 2:
                    to = x + jnp.where(t[dim] < x, 1, -1)
                    cond = (to >= 0) & (to < length)
                    out.append((self.moved(dim, to), cond, self.slot(h, lvl, t, False)))
            elif length == 2:
                out.append((self.moved(dim, 1 - x), None, self.slot(h, lvl, t, False)))
            else:
                out.append((self.moved(dim, x + 1), x < length - 1, self.slot(h, lvl, t, False)))
                out.append((self.moved(dim, x - 1), x > 0, self.slot(h, lvl, t, True)))
        return out

    def slot(self, h, lvl, t, extra):
        order = ORDERS[h]
        prefix, before = 0, 1
        for dim in order[:lvl]:
            prefix = prefix * self.dims[dim] + t[dim]
            before *= self.dims[dim]
        length = self.dims[order[lvl]]
        base = self.base[h][lvl]
        if length == 2:
            return base + prefix
        main = base + prefix * length + t[order[lvl]]
        other = base + before * length + prefix
        if isinstance(extra, bool):
            return other if extra else main
        return jnp.where(extra, other, main)

    def parent(self, h, e):
        t, lvl = self.token(h, e), self.top(e)
        dim = ORDERS[h][lvl]
        x = self.my[dim]
        to = 1 - x if self.dims[dim] == 2 else x + jnp.where(t[dim] > x, 1, -1)
        extra = False if self.dims[dim] == 2 else (to == t[dim]) & (x < to)
        return self.moved(dim, to), self.slot(h, lvl, t, extra)


def when(cond, act):
    if cond is None:
        act()
    else:
        pl.when(cond)(act)


def normalize(rows, gain):
    square = jnp.mean(rows * rows, axis=-1, keepdims=True)
    return (rows * lax.rsqrt(square + epsilon) * gain).astype(BF16)


def gated_tile(x, gate, up):
    width = gate.shape[1]
    both = jnp.dot(x, jnp.concatenate([gate, up], axis=1), preferred_element_type=F32)
    g, u = both[:, :width], both[:, width:]
    return (g / (1.0 + jnp.exp(-g)) * u).astype(BF16)


def gated(x_ref, rows, gate_ref, up_ref, out_ref, out_rows, offset):
    width = gate_ref.shape[-1]
    if width % 128:
        x = x_ref[rows, :]
        g = jnp.dot(x, gate_ref[...], preferred_element_type=F32)
        u = jnp.dot(x, up_ref[...], preferred_element_type=F32)
        out_ref[out_rows, offset : offset + width] = (g / (1.0 + jnp.exp(-g)) * u).astype(BF16)
        return

    @pl.loop(0, width // 128)
    def _(j):
        cols = pl.ds(pl.multiple_of(j * 128, 128), 128)
        to = pl.ds(pl.multiple_of(offset + j * 128, 128), 128)
        out_ref[out_rows, to] = gated_tile(x_ref[rows, :], gate_ref[:, cols], up_ref[:, cols])


def routed_kernel(
    n, dims, *refs
):
    (tok_hbm, gain, lg_hbm, lu_hbm, ld_hbm, hg_hbm, hu_hbm, hd_hbm, idx, mask) = refs[:10]
    (base_hbm, heavy_ref) = refs[10:12]
    (tok, normed, lg, lu, ld, hg, hu, hd, hidden, hhidden, picked, rows_in, rows_out, back) = refs[12:26]
    (load_sem, pair_send, pair_recv, store_sem, g_send, g_recv, s_send, s_recv) = refs[26:]
    count, width = tok.shape
    cap = picked.shape[0]
    half = width // 2
    part = lg.shape[2]
    me, core = lax.axis_index("light"), lax.axis_index("pair")
    plan = Plan(dims, me)
    chunk = 256

    loads = [
        pltpu.make_async_copy(s, d, load_sem.at[i])
        for i, (s, d) in enumerate(
            [
                (tok_hbm, tok),
                (lg_hbm, lg.at[0]),
                (lu_hbm, lu.at[0]),
                (hg_hbm, hg),
                (hu_hbm, hu),
                (hd_hbm, hd),
                (ld_hbm, ld.at[0:part]),
            ]
        )
    ]
    for copy in loads:
        copy.start()

    barrier = pltpu.get_barrier_semaphore()
    neighbours = [({"pair": 1 - core}, None)]
    for dim, length in enumerate(dims):
        x = plan.my[dim]
        if length == 2:
            neighbours.append(({"light": plan.index(plan.moved(dim, 1 - x))}, None))
        elif length > 2:
            neighbours.append(({"light": plan.index(plan.moved(dim, x + 1))}, x < length - 1))
            neighbours.append(({"light": plan.index(plan.moved(dim, x - 1))}, x > 0))
    total = 0
    for device, cond in neighbours:
        when(
            cond,
            lambda device=device: pl.semaphore_signal(
                barrier, inc=1, device_id=device, device_id_type=MESH
            ),
        )
        total = total + (1 if cond is None else jnp.where(cond, 1, 0))
    pl.semaphore_wait(barrier, total)

    swaps = [
        pltpu.make_async_remote_copy(
            src_ref=s,
            dst_ref=d,
            send_sem=pair_send.at[i],
            recv_sem=pair_recv.at[i],
            device_id={"pair": 1 - core},
            device_id_type=MESH,
        )
        for i, (s, d) in enumerate(
            [(lg_hbm, lg.at[1]), (lu_hbm, lu.at[1]), (ld_hbm, ld.at[part : 2 * part])]
        )
    ]

    loads[0].wait()

    row_id = lax.broadcasted_iota(jnp.int32, (cap, count), 1)
    taking = jnp.where((row_id == idx[...]) & (mask[...] == 1), 1.0, 0.0).astype(BF16)
    for j in range(width // 512):
        cols = slice(j * 512, (j + 1) * 512)
        picked[:, cols] = jnp.dot(taking, tok[:, cols], preferred_element_type=F32)

    def rows_of(t):
        return pl.ds(pl.multiple_of(plan.place(t, plan.my) * cap, cap), cap)

    mine = rows_of(plan.my)
    rows_in[mine, :] = normalize(picked[...], gain[...])

    sends = []

    def spread(h, e):
        t = plan.token(h, e)
        cols = pl.ds(h * half, half)
        for to, cond, _ in plan.children(h, e):
            target = pl.ds(pl.multiple_of(plan.place(t, to) * cap, cap), cap)
            copy = pltpu.make_async_remote_copy(
                src_ref=rows_in.at[rows_of(t), cols],
                dst_ref=rows_in.at[target, cols],
                send_sem=g_send.at[len(sends)],
                recv_sem=g_recv.at[h, plan.index(t)],
                device_id={"light": plan.index(to)},
                device_id_type=MESH,
            )
            when(cond, copy.start)
            sends.append((copy, cond))

    def arrive(h, e):
        t = plan.token(h, e)
        view = rows_in.at[rows_of(t), pl.ds(h * half, half)]
        pltpu.make_async_copy(view, view, g_recv.at[h, plan.index(t)]).wait()

    own = (0, 0, 0)
    for h in range(2):
        spread(h, own)
    for copy in swaps:
        copy.start()

    def norm_piece(i):
        @pl.loop(0, chunk // 32)
        def _(r):
            rows = pl.ds(pl.multiple_of(i * chunk + r * 32, 32), 32)
            normed[rows, :] = normalize(tok[rows, :].astype(F32), gain[...])

    def gated_piece(i, side):
        if i == 0:
            if side == 0:
                loads[1].wait()
                loads[2].wait()
            else:
                swaps[0].wait_recv()
                swaps[1].wait_recv()
        rows = pl.ds(i * chunk, chunk)
        gated(normed, rows, lg.at[side], lu.at[side], hidden, rows, side * part)

    stores = []

    def down_piece(i):
        if i == 0:
            loads[6].wait()
            swaps[2].wait_recv()
        rows = pl.ds(i * chunk, chunk)

        @pl.loop(0, width // 256)
        def _(j):
            cols = pl.ds(pl.multiple_of(j * 256, 256), 256)
            out = jnp.dot(hidden[rows, :], ld[:, cols], preferred_element_type=F32)
            tok[rows, cols] = (tok[rows, cols].astype(F32) + out).astype(BF16)

        copy = pltpu.make_async_copy(tok.at[rows], base_hbm.at[rows], store_sem.at[i])
        copy.start()
        stores.append(copy)

    chunks = count // chunk
    before = []
    for i in range(chunks):
        before += [functools.partial(norm_piece, i), functools.partial(gated_piece, i, 0)]
    after = [functools.partial(gated_piece, i, 1) for i in range(chunks)]
    after += [functools.partial(down_piece, i) for i in range(chunks)]

    events = [plan.events(h) for h in range(2)]
    inners = [[e for e in events[h] if e[2] == 0] for h in range(2)]
    outers = [[e for e in events[h] if e[2]] for h in range(2)]

    steps = max(len(x) for x in inners)
    for s in range(max(steps, len(before))):
        if s < len(before):
            before[s]()
        for h in range(2):
            if s < len(inners[h]):
                arrive(h, inners[h][s])
                spread(h, inners[h][s])

    blocks = n * cap
    size = min(chunk, blocks)
    parts = blocks // size
    known = dims[1] <= 2 and dims[2] <= 2

    def part_of(h, e):
        if not known:
            return None
        rel = [0, 0, 0]
        for lvl, dim in enumerate(ORDERS[h]):
            rel[dim] = e[lvl]
        groups = dims[1] * dims[2]
        rank = (rel[1] * dims[2] + rel[2] + groups - 1) % groups
        return rank * dims[0] * cap // size

    def heavy_part(k):
        if k == 0:
            loads[3].wait()
            loads[4].wait()
            loads[5].wait()
        rows = pl.ds(k * size, size)
        gated(rows_in, rows, hg, hu, hhidden, pl.ds(0, size), 0)

        @pl.loop(0, width // 256)
        def _(j):
            cols = pl.ds(pl.multiple_of(j * 256, 256), 256)
            out = jnp.dot(hhidden[...], hd[:, cols], preferred_element_type=F32)
            rows_out[rows, cols] = out.astype(BF16)

    returns = []

    def collect(h, e):
        t = plan.token(h, e)
        rows, cols = rows_of(t), pl.ds(h * half, half)
        for _, cond, slot in plan.children(h, e):

            def take(slot=slot):
                view = back.at[h, slot]
                pltpu.make_async_copy(view, view, s_recv.at[h, slot]).wait()
                added = rows_out[rows, cols].astype(F32) + view[...].astype(F32)
                rows_out[rows, cols] = added.astype(BF16)

            when(cond, take)
        if plan.top(e) < 0:
            heavy_ref[:, cols] = rows_out[rows, cols]
            return
        to, slot = plan.parent(h, e)
        copy = pltpu.make_async_remote_copy(
            src_ref=rows_out.at[rows, cols],
            dst_ref=back.at[h, slot],
            send_sem=s_send.at[len(returns)],
            recv_sem=s_recv.at[h, slot],
            device_id={"light": plan.index(to)},
            device_id_type=MESH,
        )
        copy.start()
        returns.append(copy)

    arrived, returned = set(), set()
    for k in range(parts):
        for s in range(max(len(x) for x in outers)):
            for h in range(2):
                if s < len(outers[h]) and (h, outers[h][s]) not in arrived:
                    e = outers[h][s]
                    if part_of(h, e) in (None, k):
                        arrived.add((h, e))
                        arrive(h, e)
                        spread(h, e)
        heavy_part(k)
        if k == parts - 1 or known:
            for s in range(max(len(x) for x in outers)):
                for h in range(2):
                    if s < len(outers[h]):
                        e = outers[h][-1 - s]
                        if (h, e) not in returned and (k == parts - 1 or part_of(h, e) == k):
                            returned.add((h, e))
                            collect(h, e)

    for s in range(max(steps, len(after))):
        if s < len(after):
            after[s]()
        for h in range(2):
            if s < len(inners[h]):
                collect(h, inners[h][-1 - s])
    for h in range(2):
        collect(h, own)

    for copy, cond in sends:
        when(cond, copy.wait_send)
    for copy in returns:
        copy.wait_send()
    for copy in swaps:
        copy.wait_send()
    for copy in stores:
        copy.wait()


def place_kernel(base, heavy, idx, mask, out):
    rows, cap = base.shape[0], idx.shape[1]
    row_id = lax.broadcasted_iota(jnp.int32, (rows, cap), 0) + pl.program_id(0) * rows
    placing = jnp.where((row_id == idx[...]) & (mask[...] == 1), 1.0, 0.0).astype(BF16)
    added = jnp.dot(placing, heavy[...], preferred_element_type=F32)
    out[...] = (base[...].astype(F32) + added).astype(BF16)


def edge_counts(dims):
    plan = Plan(dims, 0)
    return [
        sum(len(plan.children(h, e)) for e in [(0, 0, 0)] + plan.events(h)) for h in range(2)
    ], plan.slots


def body(
    n,
    tokens,
    norm_gain,
    light_gate,
    light_up,
    light_down,
    heavy_gate,
    heavy_up,
    heavy_down,
    slot_token_index,
    slot_active_mask,
):
    count, width = tokens.shape
    cap = slot_token_index.shape[0]
    part, heavy = light_gate.shape[1], heavy_gate.shape[1]
    dims = three_factors(n)
    edges, slots = edge_counts(dims)
    blocks = n * cap
    hbm = pl.BlockSpec(memory_space=pl.ANY)
    vmem = pl.BlockSpec(memory_space=pltpu.VMEM)
    dma = pltpu.SemaphoreType.DMA
    base, rows = pl.pallas_call(
        functools.partial(routed_kernel, n, dims),
        out_shape=(
            jax.ShapeDtypeStruct((count, width), BF16),
            jax.ShapeDtypeStruct((cap, width), BF16),
        ),
        in_specs=[hbm, vmem] + [hbm] * 6 + [vmem] * 2,
        out_specs=(hbm, vmem),
        scratch_shapes=[
            pltpu.VMEM((count, width), BF16),
            pltpu.VMEM((count, width), BF16),
            pltpu.VMEM((2, width, part), BF16),
            pltpu.VMEM((2, width, part), BF16),
            pltpu.VMEM((2 * part, width), BF16),
            pltpu.VMEM((width, heavy), BF16),
            pltpu.VMEM((width, heavy), BF16),
            pltpu.VMEM((heavy, width), BF16),
            pltpu.VMEM((count, 2 * part), BF16),
            pltpu.VMEM((min(256, blocks), heavy), BF16),
            pltpu.VMEM((cap, width), F32),
            pltpu.VMEM((blocks, width), BF16),
            pltpu.VMEM((blocks, width), BF16),
            pltpu.VMEM((2, max(slots), cap, width // 2), BF16),
            dma((7,)),
            dma((3,)),
            dma((3,)),
            dma((count // 256,)),
            dma((sum(edges),)),
            dma((2, n)),
            dma((2 * (n - 1),)),
            dma((2, max(slots))),
        ],
        compiler_params=pltpu.CompilerParams(
            collective_id=0, has_side_effects=True, vmem_limit_bytes=62 * 2**20
        ),
    )(
        tokens,
        norm_gain.astype(F32)[None, :],
        light_gate,
        light_up,
        light_down,
        heavy_gate,
        heavy_up,
        heavy_down,
        slot_token_index[:, None],
        slot_active_mask[:, None],
    )
    tile = 256
    return pl.pallas_call(
        place_kernel,
        grid=(count // tile,),
        out_shape=jax.ShapeDtypeStruct((count, width), BF16),
        in_specs=[
            pl.BlockSpec((tile, width), lambda i: (i, 0)),
            pl.BlockSpec((cap, width), lambda i: (0, 0)),
            pl.BlockSpec((1, cap), lambda i: (0, 0)),
            pl.BlockSpec((1, cap), lambda i: (0, 0)),
        ],
        out_specs=pl.BlockSpec((tile, width), lambda i: (i, 0)),
    )(base, rows, slot_token_index[None, :], slot_active_mask[None, :])


def solution(mesh):
    placed = (
        P(("light", "pair"), None),
        P(),
        P(None, "pair"),
        P(None, "pair"),
        P("pair", None),
        P(None, "light"),
        P(None, "light"),
        P("light", None),
        P(("light", "pair")),
        P(("light", "pair")),
    )
    return jax.shard_map(
        functools.partial(body, mesh.shape["light"]),
        mesh=mesh,
        in_specs=placed,
        out_specs=P(("light", "pair"), None),
        check_vma=False,
    )
```

time: 245 us -> 74.9 us (0.31)
  waiting for transfers between devices: 158 us -> 0 us
  Pallas kernels: 0 us -> 71.9 us
  matrix products: 58.5 us -> 0 us
  between operations: 13.2 us -> 0.01 us
  other arithmetic: 9.61 us -> 0 us
    reduce_scatter x2 -> x0, waiting for transfers between devices: 92.3 us -> none  [the longest x1 62.1 us: body(): lax.psum_scatter(jnp.dot(heavy_hidden, heavy_down, preferred_element_type...]
    pallas_call x0 -> x2, Pallas kernels: none -> 71.9 us  [the longest x1 66.4 us: body(): pl.pallas_call(functools.partial(routed_kernel, n, dims), out_shape=(jax....]
    all_gather x2 -> x0, waiting for transfers between devices: 64.7 us -> none  [the longest x1 61.3 us: body(): lax.all_gather(routed_output, 'light', axis=0, tiled=True)]
    dot_general x5 -> x0, matrix products: 58.5 us -> none  [the longest x1 22.2 us: body(): jnp.dot(light_hidden, light_down, preferred_element_type=jnp.float32)]
    convert_element_type x2 -> x0, other arithmetic: 3.74 us -> none  [the longest x1 3.05 us: body(): (residual * lax.rsqrt(mean_square + epsilon) * norm_gain).astype(jnp.bflo...]
    gather x1 -> x0, local copies, waits for them, and re-layouts: 3.49 us -> none  [body(): jnp.take(normalized_input, slot_token_index, axis=0) * active_flags]
    reduce_sum x1 -> x0, other arithmetic: 3.07 us -> none  [body(): mean_square = jnp.mean(residual * residual, axis=-1, keepdims=True)]
    broadcast_in_dim x0 -> x2, local copies, waits for them, and re-layouts: none -> 2.67 us  [the longest x1 1.34 us: body(): slot_token_index[:, None]]
  transfers between devices with their start and end apart: 4 -> 0, of which waited for: 4 -> 0; matrix products, arithmetic and copies ran while one was open for 21% -> 0% of each run, Pallas kernels for 0% -> 0%
where the time goes in v1:
time: 74.9 us; the launch traced here: 74.6 us
  Pallas kernels  71.9 us (96%)
  local copies, waits for them, and re-layouts  2.67 us (4%)
    pallas_call x1, Pallas kernels, body(): pl.pallas_call(functools.partial(routed_kernel, n, dims), out_shape=(jax....  66.4 us
    pallas_call x1, Pallas kernels, body(): pl.pallas_call(place_kernel, grid=(count // tile,), out_shape=jax.ShapeDt...  5.47 us

profile of v1, /device:TPU:8, one launch (start us, length us, event | category | flops | bytes accessed | tf_op | source)
XLA Modules:
  0.0 74.6 jit_solution(6044868766765343527)
XLA Ops:
  0.0 1.3 %copy.12.refs_9_ = s32[32,1]{1,0:T(8,128)} copy(s32[32,1]{0,1:T(1,128)} %bitcast.8) | data formatting | bytes 256 | tf_op jit(solution)/shard_map/broadcast_in_dim | solution.py:506
  1.3 1.3 %copy.11.refs_8_ = s32[32,1]{1,0:T(8,128)} copy(s32[32,1]{0,1:T(1,128)} %bitcast.6) | data formatting | bytes 256 | tf_op jit(solution)/shard_map/broadcast_in_dim | solution.py:505
  2.7 66.4 %shard_map.100 = (bf16[1024,2048]{1,0:T(8,128)(2,1)}, bf16[32,2048]{1,0:T(8,128)(2,1)}) custom-call(bf16[1024,2048]{1,0:T(8,128)(2,1)} %refs_0_.1, f32[1,2048]{1,0:T(1,128)} %bitcast.5, bf16[2048,640]{1,0:T(8,128)(2,1)} %refs_2_.1, bf16[2048,640]{1,0:T(8,128)(2,1)} %refs_3_.1, bf16[640,2048]{1,0:T(8,128)(2,1)} %refs_4_.1, bf16[2048,640]{1,0:T(8,128)(2,1)} %refs_5_.1, ...), custom_call_target="tpu_custom_call" | custom-call | tf_op jit(solution)/shard_map/pallas_call | solution.py:461
  69.1 5.5 %shard_map.101 = bf16[1024,2048]{1,0:T(8,128)(2,1)} custom-call(bf16[1024,2048]{1,0:T(8,128)(2,1)} %get-tuple-element.7.base, bf16[32,2048]{1,0:T(8,128)(2,1)} %get-tuple-element.8.heavy, s32[1,32]{1,0:T(1,128)} %bitcast.7, s32[1,32]{1,0:T(1,128)} %bitcast.9), custom_call_target="tpu_custom_call" | custom-call | tf_op jit(solution)/shard_map/pallas_call | solution.py:509

commit v2 on v1

--- a/solution.py
+++ b/solution.py
@@ -189,8 +189,7 @@
             ]
         )
     ]
-    for copy in loads:
-        copy.start()
+    loads[0].start()
 
     barrier = pltpu.get_barrier_semaphore()
     neighbours = [({"pair": 1 - core}, None)]
@@ -227,9 +226,16 @@
     ]
 
     loads[0].wait()
-
-    row_id = lax.broadcasted_iota(jnp.int32, (cap, count), 1)
-    taking = jnp.where((row_id == idx[...]) & (mask[...] == 1), 1.0, 0.0).astype(BF16)
+    for copy in loads[1:]:
+        copy.start()
+
+    live = jnp.where(mask[...] == 1, idx[...], -1).astype(F32)
+    diagonal = lax.broadcasted_iota(jnp.int32, (cap, cap), 0) == lax.broadcasted_iota(
+        jnp.int32, (cap, cap), 1
+    )
+    wanted = jnp.sum(jnp.where(diagonal, live, 0.0), axis=1, keepdims=True)
+    row_id = lax.broadcasted_iota(jnp.int32, (cap, count), 1).astype(F32)
+    taking = jnp.where(row_id == wanted, 1.0, 0.0).astype(BF16)
     for j in range(width // 512):
         cols = slice(j * 512, (j + 1) * 512)
         picked[:, cols] = jnp.dot(taking, tok[:, cols], preferred_element_type=F32)
@@ -275,41 +281,48 @@
             rows = pl.ds(pl.multiple_of(i * chunk + r * 32, 32), 32)
             normed[rows, :] = normalize(tok[rows, :].astype(F32), gain[...])
 
-    def gated_piece(i, side):
-        if i == 0:
+    tall = 512 if count % 512 == 0 else chunk
+
+    def gated_piece(j, side):
+        if j == 0:
             if side == 0:
                 loads[1].wait()
                 loads[2].wait()
             else:
                 swaps[0].wait_recv()
                 swaps[1].wait_recv()
-        rows = pl.ds(i * chunk, chunk)
-        gated(normed, rows, lg.at[side], lu.at[side], hidden, rows, side * part)
+        cols = slice(j * 128, (j + 1) * 128)
+        to = slice(side * part + j * 128, side * part + (j + 1) * 128)
+
+        @pl.loop(0, count // tall)
+        def _(r):
+            rows = pl.ds(pl.multiple_of(r * tall, tall), tall)
+            hidden[rows, to] = gated_tile(normed[rows, :], lg[side, :, cols], lu[side, :, cols])
 
     stores = []
+    wide = width // store_sem.shape[0]
 
     def down_piece(i):
         if i == 0:
             loads[6].wait()
             swaps[2].wait_recv()
-        rows = pl.ds(i * chunk, chunk)
-
-        @pl.loop(0, width // 256)
-        def _(j):
-            cols = pl.ds(pl.multiple_of(j * 256, 256), 256)
+
+        @pl.loop(0, (count // tall) * (wide // 256))
+        def _(k):
+            rows = pl.ds(pl.multiple_of(k % (count // tall) * tall, tall), tall)
+            cols = pl.ds(pl.multiple_of(i * wide + k // (count // tall) * 256, 256), 256)
             out = jnp.dot(hidden[rows, :], ld[:, cols], preferred_element_type=F32)
             tok[rows, cols] = (tok[rows, cols].astype(F32) + out).astype(BF16)
 
-        copy = pltpu.make_async_copy(tok.at[rows], base_hbm.at[rows], store_sem.at[i])
+        cols = pl.ds(i * wide, wide)
+        copy = pltpu.make_async_copy(tok.at[:, cols], base_hbm.at[:, cols], store_sem.at[i])
         copy.start()
         stores.append(copy)
 
-    chunks = count // chunk
-    before = []
-    for i in range(chunks):
-        before += [functools.partial(norm_piece, i), functools.partial(gated_piece, i, 0)]
-    after = [functools.partial(gated_piece, i, 1) for i in range(chunks)]
-    after += [functools.partial(down_piece, i) for i in range(chunks)]
+    before = [functools.partial(norm_piece, i) for i in range(count // chunk)]
+    before += [functools.partial(gated_piece, j, 0) for j in range(part // 128)]
+    after = [functools.partial(gated_piece, j, 1) for j in range(part // 128)]
+    after += [functools.partial(down_piece, i) for i in range(store_sem.shape[0])]
 
     events = [plan.events(h) for h in range(2)]
     inners = [[e for e in events[h] if e[2] == 0] for h in range(2)]
@@ -484,7 +497,7 @@
             dma((7,)),
             dma((3,)),
             dma((3,)),
-            dma((count // 256,)),
+            dma((width // 512,)),
             dma((sum(edges),)),
             dma((2, n)),
             dma((2 * (n - 1),)),
@@ -502,8 +515,8 @@
         heavy_gate,
         heavy_up,
         heavy_down,
-        slot_token_index[:, None],
-        slot_active_mask[:, None],
+        slot_token_index[None, :],
+        slot_active_mask[None, :],
     )
     tile = 256
     return pl.pallas_call(

time: 74.9 us -> 69.6 us (0.929)
  local copies, waits for them, and re-layouts: 2.67 us -> 0 us
  Pallas kernels: 71.9 us -> 69.3 us
    broadcast_in_dim x2 -> x0, local copies, waits for them, and re-layouts: 2.67 us -> none  [the longest x1 1.34 us: body(): slot_token_index[:, None]]
    pallas_call x1, Pallas kernels: 66.4 us -> 63.9 us  [body(): pl.pallas_call(functools.partial(routed_kernel, n, dims), out_shape=(jax....]
where the time goes in v2:
time: 69.6 us; the launch traced here: 69.3 us
  Pallas kernels  69.3 us (100%)
    pallas_call x1, Pallas kernels, body(): pl.pallas_call(functools.partial(routed_kernel, n, dims), out_shape=(jax....  63.9 us
    pallas_call x1, Pallas kernels, body(): pl.pallas_call(place_kernel, grid=(count // tile,), out_shape=jax.ShapeDt...  5.47 us

profile of v2, /device:TPU:8, one launch (start us, length us, event | category | flops | bytes accessed | tf_op | source)
XLA Modules:
  0.0 69.3 jit_solution(126005136655230017)
XLA Ops:
  0.0 63.9 %shard_map.100 = (bf16[1024,2048]{1,0:T(8,128)(2,1)}, bf16[32,2048]{1,0:T(8,128)(2,1)}) custom-call(bf16[1024,2048]{1,0:T(8,128)(2,1)} %refs_0_.1, f32[1,2048]{1,0:T(1,128)} %bitcast.3, bf16[2048,640]{1,0:T(8,128)(2,1)} %refs_2_.1, bf16[2048,640]{1,0:T(8,128)(2,1)} %refs_3_.1, bf16[640,2048]{1,0:T(8,128)(2,1)} %refs_4_.1, bf16[2048,640]{1,0:T(8,128)(2,1)} %refs_5_.1, ...), custom_call_target="tpu_custom_call" | custom-call | tf_op jit(solution)/shard_map/pallas_call | solution.py:474
  63.9 5.5 %shard_map.101 = bf16[1024,2048]{1,0:T(8,128)(2,1)} custom-call(bf16[1024,2048]{1,0:T(8,128)(2,1)} %get-tuple-element.7.base, bf16[32,2048]{1,0:T(8,128)(2,1)} %get-tuple-element.8.heavy, s32[1,32]{1,0:T(1,128)} %bitcast.5, s32[1,32]{1,0:T(1,128)} %bitcast.7), custom_call_target="tpu_custom_call" | custom-call | tf_op jit(solution)/shard_map/pallas_call | solution.py:522

commit v3 on v2

--- a/solution.py
+++ b/solution.py
@@ -10,7 +10,7 @@
 epsilon = 1e-06
 MESH = pl.DeviceIdType.MESH
 F32, BF16 = jnp.float32, jnp.bfloat16
-ORDERS = ((0, 1, 2), (0, 2, 1))
+ORDERS = ((0, 1, 2), (2, 0, 1))
 
 
 def three_factors(n):
@@ -125,6 +125,10 @@
         return self.moved(dim, to), self.slot(h, lvl, t, extra)
 
 
+def first_columns(width):
+    return width * 5 // 8 // 128 * 128
+
+
 def when(cond, act):
     if cond is None:
         act()
@@ -169,7 +173,8 @@
     (load_sem, pair_send, pair_recv, store_sem, g_send, g_recv, s_send, s_recv) = refs[26:]
     count, width = tok.shape
     cap = picked.shape[0]
-    half = width // 2
+    first = first_columns(width)
+    columns = (pl.ds(0, first), pl.ds(first, width - first))
     part = lg.shape[2]
     me, core = lax.axis_index("light"), lax.axis_index("pair")
     plan = Plan(dims, me)
@@ -250,7 +255,7 @@
 
     def spread(h, e):
         t = plan.token(h, e)
-        cols = pl.ds(h * half, half)
+        cols = columns[h]
         for to, cond, _ in plan.children(h, e):
             target = pl.ds(pl.multiple_of(plan.place(t, to) * cap, cap), cap)
             copy = pltpu.make_async_remote_copy(
@@ -266,7 +271,7 @@
 
     def arrive(h, e):
         t = plan.token(h, e)
-        view = rows_in.at[rows_of(t), pl.ds(h * half, half)]
+        view = rows_in.at[rows_of(t), columns[h]]
         pltpu.make_async_copy(view, view, g_recv.at[h, plan.index(t)]).wait()
 
     own = (0, 0, 0)
@@ -370,11 +375,11 @@
 
     def collect(h, e):
         t = plan.token(h, e)
-        rows, cols = rows_of(t), pl.ds(h * half, half)
+        rows, cols = rows_of(t), columns[h]
         for _, cond, slot in plan.children(h, e):
 
             def take(slot=slot):
-                view = back.at[h, slot]
+                view = back.at[h, slot, :, pl.ds(0, cols.size)]
                 pltpu.make_async_copy(view, view, s_recv.at[h, slot]).wait()
                 added = rows_out[rows, cols].astype(F32) + view[...].astype(F32)
                 rows_out[rows, cols] = added.astype(BF16)
@@ -386,7 +391,7 @@
         to, slot = plan.parent(h, e)
         copy = pltpu.make_async_remote_copy(
             src_ref=rows_out.at[rows, cols],
-            dst_ref=back.at[h, slot],
+            dst_ref=back.at[h, slot, :, pl.ds(0, cols.size)],
             send_sem=s_send.at[len(returns)],
             recv_sem=s_recv.at[h, slot],
             device_id={"light": plan.index(to)},
@@ -493,7 +498,7 @@
             pltpu.VMEM((cap, width), F32),
             pltpu.VMEM((blocks, width), BF16),
             pltpu.VMEM((blocks, width), BF16),
-            pltpu.VMEM((2, max(slots), cap, width // 2), BF16),
+            pltpu.VMEM((2, max(slots), cap, first_columns(width)), BF16),
             dma((7,)),
             dma((3,)),
             dma((3,)),

time: 69.6 us -> 70.5 us (1.013)
  Pallas kernels: 69.3 us -> 70.2 us
    pallas_call x1, Pallas kernels: 63.9 us -> 64.7 us  [body(): pl.pallas_call(functools.partial(routed_kernel, n, dims), out_shape=(jax....]
where the time goes in v3:
time: 70.5 us; the launch traced here: 70.2 us
  Pallas kernels  70.2 us (100%)
    pallas_call x1, Pallas kernels, body(): pl.pallas_call(functools.partial(routed_kernel, n, dims), out_shape=(jax....  64.7 us
    pallas_call x1, Pallas kernels, body(): pl.pallas_call(place_kernel, grid=(count // tile,), out_shape=jax.ShapeDt...  5.47 us

profile of v3, /device:TPU:8, one launch (start us, length us, event | category | flops | bytes accessed | tf_op | source)
XLA Modules:
  0.0 70.2 jit_solution(9256640131870099048)
XLA Ops:
  0.0 64.7 %shard_map.100 = (bf16[1024,2048]{1,0:T(8,128)(2,1)}, bf16[32,2048]{1,0:T(8,128)(2,1)}) custom-call(bf16[1024,2048]{1,0:T(8,128)(2,1)} %refs_0_.1, f32[1,2048]{1,0:T(1,128)} %bitcast.3, bf16[2048,640]{1,0:T(8,128)(2,1)} %refs_2_.1, bf16[2048,640]{1,0:T(8,128)(2,1)} %refs_3_.1, bf16[640,2048]{1,0:T(8,128)(2,1)} %refs_4_.1, bf16[2048,640]{1,0:T(8,128)(2,1)} %refs_5_.1, ...), custom_call_target="tpu_custom_call" | custom-call | tf_op jit(solution)/shard_map/pallas_call | solution.py:479
  64.8 5.5 %shard_map.101 = bf16[1024,2048]{1,0:T(8,128)(2,1)} custom-call(bf16[1024,2048]{1,0:T(8,128)(2,1)} %get-tuple-element.7.base, bf16[32,2048]{1,0:T(8,128)(2,1)} %get-tuple-element.8.heavy, s32[1,32]{1,0:T(1,128)} %bitcast.5, s32[1,32]{1,0:T(1,128)} %bitcast.7), custom_call_target="tpu_custom_call" | custom-call | tf_op jit(solution)/shard_map/pallas_call | solution.py:527
